TPU v7x, 32 devices: a whole 2x2x4 slice. The times are simulated.
32 devices in a mesh: feat: 8 (over y, x, core), node: 4 (over z).
Axes of the slice: x: 2, y: 2, z: 4, core: 2. Of those that a mesh axis runs over, the one named last changes fastest.
Arguments:
- features: bfloat16 [4, 512, 16384], P('node', 'feat'), may hold values from -6 to 6
- target_ids: int32 [4, 4096], P('node'), may hold values from 0 to 16383
- block_ids: int32 [4, 32, 8], P('node'), may hold values from 0 to 127
- tile_counts: int32 [4, 32], P('node'), may hold values from 1 to 8, as said below
- adjacency: bfloat16 [4, 32, 8, 128, 128], P('node'), may hold values from 0 to 0.25
- w_neigh: bfloat16 [256, 512], P(None, 'feat'), may hold values from -0.1875 to 0.1875
- w_self: bfloat16 [256, 512], P(None, 'feat'), may hold values from -0.1875 to 0.1875
- w_head: bfloat16 [256, 256], replicated, may hold values from -0.375 to 0.375
- grad_scores: bfloat16 [4, 4096, 256], P('node', 'feat'), may hold values from -6 to 6
Outputs:
- scores: bfloat16 [4, 4096, 256], P('node', 'feat')
- grad_head: float32 [256, 256], replicated
- grad_neigh: float32 [256, 512], P(None, 'feat')
- grad_self: float32 [256, 512], P(None, 'feat')
Inputs may be any that keep to these rules, and one draw needn't show every extreme that they name: `tile_counts`: one group, drawn from the seed, has all of its tiles at 8 live slots; every tile of the other groups has fewer than 8.
All inputs are finite; a program needn't handle non-finite values.
Results may differ from a plain program's by a relative error of at most 0.0056.
Values may be sent and summed in bfloat16 or wider, within the bound.
A program may use at most 64 MiB of HBM per device.

v0:
```python
import jax
import jax.numpy as jnp
from jax import lax
from jax.sharding import PartitionSpec as P


def aggregate_local(feature_rows, block_row, count_row, adjacency_group):
    width = feature_rows.shape[0]
    tiles = block_row.shape[0]
    slots = block_row.shape[1]
    blocks = feature_rows.reshape(width, -1, 128)
    gathered = jnp.take(blocks, block_row.reshape(-1), axis=1).reshape(width, tiles, slots, 128)
    live = (jnp.arange(slots, dtype=jnp.int32)[None, :] < count_row[:, None]).astype(jnp.bfloat16)
    masked = gathered * live[None, :, :, None]
    summed = jnp.einsum(
        "tkrs,ftks->ftr", adjacency_group, masked, preferred_element_type=jnp.float32
    )
    summed = summed / count_row.astype(jnp.float32)[None, :, None]
    return summed.astype(jnp.bfloat16).reshape(width, tiles * 128)


def contract_first(left, right):
    return lax.dot_general(
        left, right, (((0,), (1,)), ((), ())), preferred_element_type=jnp.float32
    )


def body(
    features, target_ids, block_ids, tile_counts, adjacency, w_neigh, w_self, w_head, grad_scores
):
    feature_rows = features[0]
    aggregate = aggregate_local(feature_rows, block_ids[0], tile_counts[0], adjacency[0])
    own = jnp.take(feature_rows, target_ids[0], axis=1)
    agg_part = aggregate
    own_part = own
    preact = lax.psum_scatter(
        contract_first(agg_part, w_neigh) + contract_first(own_part, w_self),
        "feat",
        scatter_dimension=0,
        tiled=True,
    )
    hidden = jax.nn.silu(preact).astype(jnp.bfloat16)
    scores = jnp.dot(hidden, w_head.T, preferred_element_type=jnp.float32).astype(jnp.bfloat16)
    cotangent = grad_scores[0]
    head_local = lax.dot_general(
        cotangent, hidden, (((0,), (0,)), ((), ())), preferred_element_type=jnp.float32
    )
    grad_head = lax.psum(head_local, ("feat", "node"))
    grad_hidden = jnp.dot(cotangent, w_head, preferred_element_type=jnp.float32)
    sigma = jax.nn.sigmoid(preact)
    grad_pre = (grad_hidden * sigma * (1.0 + preact * (1.0 - sigma))).astype(jnp.bfloat16)
    shard_piece = lax.all_gather(grad_pre, "feat", axis=0, tiled=True)
    agg_part = aggregate
    own_part = own
    neigh_local = contract_first(shard_piece, agg_part)
    self_local = contract_first(shard_piece, own_part)
    grad_neigh, grad_self = lax.psum((neigh_local, self_local), "node")
    return (scores[None], grad_head, grad_neigh, grad_self)


def solution(mesh):
    in_specs = (
        P("node", "feat", None),
        P("node", None),
        P("node", None, None),
        P("node", None),
        P("node", None, None, None, None),
        P(None, "feat"),
        P(None, "feat"),
        P(),
        P("node", "feat", None),
    )
    out_specs = (P("node", "feat", None), P(), P(None, "feat"), P(None, "feat"))
    return jax.shard_map(body, mesh=mesh, in_specs=in_specs, out_specs=out_specs, check_vma=False)
```

profile of v0, /device:TPU:0, one launch (start us, length us, event | category | flops | bytes accessed | tf_op | source)
XLA Modules:
  0.0 308.8 jit_solution(13335983999297234126)
XLA Ops:
  7.2 0.0 copy-start
  7.2 0.0 copy-start.1
  7.2 0.0 reduce-scatter.2.cloned.1.call-start
  7.2 0.8 compare_and_fusion.1
  8.1 0.8 copy.23
  8.8 0.7 bitcast_convert_fusion
  9.5 0.1 copy.22
  9.6 0.7 compare_select_fusion
  10.3 0.7 compare_and_fusion
  11.1 0.7 fusion.33
  11.8 0.1 reshape_squeeze.10
  11.9 4.8 %copy.26 = bf16[1,64,16384]{1,2,0:T(8,128)(2,1)} copy(bf16[1,64,16384]{2,1,0:T(8,128)(2,1)} %param.9) | data formatting | bytes 4194304 | tf_op args[0]
  16.7 0.0 copy-done.1
  16.7 0.6 copy.30
  17.3 1.4 copy.24
  18.6 3.1 gather_fusion
  21.7 13.8 %gather_fusion.1 = bf16[4096,64]{1,0:T(8,128)(2,1)S(1)} fusion(bf16[64,16384]{0,1:T(8,128)(2,1)} %bitcast.57, s32[4096]{0:T(1024)S(1)} %broadcast_clamp_fusion), kind=kCustom, calls=%fused_computation.1 | custom fusion | bytes 1064960 | tf_op jit(solution)/shard_map/jit(_take)/gather | solution.py:33
  35.5 0.0 copy-done.4
  35.5 0.0 copy-start.2
  35.5 1.5 fusion.29
  37.0 0.7 copy-done.2
  37.7 0.0 copy-start.5
  37.7 5.7 %fusion.19 = bf16[32,8,8,128]{3,2,1,0:T(8,128)(2,1)S(1)} fusion(bf16[1,32,8,128,128]{4,3,2,1,0:T(8,128)(2,1)} %param.13, bf16[64,32,8,128]{3,0,2,1:T(8,128)(2,1)S(1)} %bitcast.60, pred[32,8]{1,0:T(8,128)(4,1)S(1)} %copy.22, bf16[32,8]{1,0:T(8,128)(2,1)S(1)} %fusion.33, f32[32]{0:T(128)S(1)} %bitcast_convert_fusion), kind=kOutput, calls=%fused_computation.19 | convolution fusion | flops 541589504 | bytes 13108096 | tf_op jit(solution)/shard_map/tkrs,ftks->ftr/dot_general | solution.py:15
  43.4 0.0 copy-done.5
  43.4 2.7 convolution_add_fusion
  46.1 0.0 reduce-scatter.2.cloned.1.call-update
  46.1 0.0 all-gather.2.cloned.1.call-start
  46.2 54.1 %reduce-scatter.2.cloned.1.call-done = f32[512,256]{1,0:T(8,128)} async-done(((f32[4096,256]{1,0:T(8,128)}), f32[512,256]{1,0:T(8,128)}) %reduce-scatter.2.cloned.1.call-update) | async-done | bytes 524304 | tf_op jit(solution)/shard_map/reduce_scatter | solution.py:36
  100.3 0.0 copy-done
  100.3 0.0 copy-done.7
  100.3 2.0 fusion.13
  102.3 0.0 all-gather.2.cloned.1.call-update
  102.4 0.0 all-reduce.4.cloned.1.call-start
  102.4 2.1 convolution_bitcast_fusion
  104.5 0.0 all-reduce.4.cloned.1.call-update
  104.5 0.0 all-reduce.6.cloned.1.call-start
  104.6 26.3 %all-gather.2.cloned.1.call-done = bf16[4096,256]{1,0:T(8,128)(2,1)} async-done(((bf16[512,256]{1,0:T(8,128)(2,1)}), bf16[4096,256]{1,0:T(8,128)(2,1)}) %all-gather.2.cloned.1.call-update) | async-done | bytes 2097168 | tf_op jit(solution)/shard_map/all_gather | solution.py:52
  130.9 4.9 %fusion.30 = f32[256,64]{0,1:T(8,128)} fusion(bf16[4096,256]{1,0:T(8,128)(2,1)} %all-gather.2.cloned.1.call-done, bf16[4096,64]{1,0:T(8,128)(2,1)S(1)} %gather_fusion.1, pred[4096]{0:T(1024)(128)(4,1)S(1)} %compare_and_fusion), kind=kOutput, calls=%fused_computation.28 | convolution fusion | flops 134479872 | bytes 2691072 | tf_op jit(solution)/shard_map/dot_general | solution.py:23
  135.8 0.0 copy-done.3
  135.8 1.1 fusion.24
  136.9 0.0 all-reduce.6.cloned.1.call-update
  136.9 0.0 copy-done.6
  136.9 1.0 fusion.14
  137.9 124.9 %all-reduce.4.cloned.1.call-done = f32[256,256]{0,1:T(8,128)} async-done(((f32[256,256]{0,1:T(8,128)}), f32[256,256]{0,1:T(8,128)}) %all-reduce.4.cloned.1.call-update) | async-done | bytes 262160 | tf_op jit(solution)/shard_map/psum | solution.py:48
  262.9 1.8 copy.27
  264.6 34.7 %all-reduce.6.cloned.1.call-done = (f32[256,64]{0,1:T(8,128)}, f32[256,64]{0,1:T(8,128)}) async-done(((f32[256,64]{0,1:T(8,128)}, f32[256,64]{0,1:T(8,128)}), (f32[256,64]{0,1:T(8,128)}, f32[256,64]{0,1:T(8,128)})) %all-reduce.6.cloned.1.call-update) | async-done | bytes 131088 | tf_op jit(solution)/shard_map/psum | solution.py:57
  299.4 1.5 copy.42
  300.8 1.5 copy.43
  (7 shorter events, 0.0 us)
Async XLA Ops:
  7.2 93.1 %copy-start = (bf16[1,512,256]{2,1,0:T(8,128)(2,1)S(1)}, bf16[1,512,256]{2,1,0:T(8,128)(2,1)}, u32[]{:S(2)}) copy-start(bf16[1,512,256]{2,1,0:T(8,128)(2,1)} %param.17) | copy-start | bytes 786436
  7.2 9.5 %copy-start.1 = (bf16[1,64,16384]{2,1,0:T(8,128)(2,1)S(1)}, bf16[1,64,16384]{2,1,0:T(8,128)(2,1)}, u32[]{:S(2)}) copy-start(bf16[1,64,16384]{2,1,0:T(8,128)(2,1)} %param.9) | copy-start | bytes 6291460
  7.2 93.1 %reduce-scatter.2.cloned.1.call-start = ((), (), s32[]{:S(2)}) async-start(), calls=%async_computation.1 | async-start | bytes 4718592 | tf_op jit(solution)/shard_map/reduce_scatter | solution.py:36
  21.7 13.8 %copy-start.4 = (bf16[256,64]{0,1:T(8,128)(2,1)S(1)}, bf16[256,64]{0,1:T(8,128)(2,1)}, u32[]{:S(2)}) copy-start(bf16[256,64]{0,1:T(8,128)(2,1)} %param.15) | copy-start | bytes 98308
  35.5 2.2 copy-start.2
  37.7 5.7 %copy-start.5 = (bf16[256,64]{0,1:T(8,128)(2,1)S(1)}, bf16[256,64]{0,1:T(8,128)(2,1)}, u32[]{:S(2)}) copy-start(bf16[256,64]{0,1:T(8,128)(2,1)} %param.14) | copy-start | bytes 98308
  46.1 54.2 %copy-start.7 = (bf16[256,256]{1,0:T(8,128)(2,1)S(1)}, bf16[256,256]{1,0:T(8,128)(2,1)}, u32[]{:S(2)}) copy-start(bf16[256,256]{1,0:T(8,128)(2,1)} %param.16) | copy-start | bytes 393220
  46.1 84.7 %all-gather.2.cloned.1.call-start = ((), (), s32[]{:S(2)}) async-start(), calls=%async_computation.3 | async-start | bytes 2359296 | tf_op jit(solution)/shard_map/all_gather | solution.py:52
  102.4 160.5 %all-reduce.4.cloned.1.call-start = ((), (), s32[]{:S(2)}) async-start(), calls=%async_computation.2 | async-start | bytes 524288 | tf_op jit(solution)/shard_map/psum | solution.py:48
  104.5 32.5 %copy-start.6 = (f32[512,256]{1,0:T(8,128)S(1)}, f32[512,256]{1,0:T(8,128)}, u32[]{:S(2)}) copy-start(f32[512,256]{1,0:T(8,128)} %reduce-scatter.2.cloned.1.call-done) | copy-start | bytes 1572868
  104.5 194.9 %all-reduce.6.cloned.1.call-start = ((), (), s32[]{:S(2)}) async-start(), calls=%async_computation.4 | async-start | bytes 262144 | tf_op jit(solution)/shard_map/psum | solution.py:57
  130.8 4.9 %copy-start.3 = (bf16[4096,256]{1,0:T(8,128)(2,1)S(1)}, bf16[4096,256]{1,0:T(8,128)(2,1)}, u32[]{:S(2)}) copy-start(bf16[4096,256]{1,0:T(8,128)(2,1)} %all-gather.2.cloned.1.call-done) | copy-start | bytes 6291460
Sparse Core Ops, SparseCore 0:
  46.2 53.9 reduce-scatter.1
  102.9 27.8 all-gather.1
  137.8 124.9 all-reduce.3
  265.8 33.5 all-reduce.5
where the time goes:
time: 309 us
  waiting for transfers between devices  240 us (78%)
  local copies, waits for them, and re-layouts  30 us (10%)
  matrix products  21 us (7%)
  between operations  13.9 us (4%)
  other arithmetic  3.71 us (1%)
    psum x1, waiting for transfers between devices, body(): grad_head = lax.psum(head_local, ('feat', 'node'))  125 us
    reduce_scatter x1, waiting for transfers between devices, body(): lax.psum_scatter(contract_first(agg_part, w_neigh) + contract_first(own_p...  54.1 us
    psum x1, waiting for transfers between devices, body(): grad_neigh, grad_self = lax.psum((neigh_local, self_local), 'node')  34.7 us
    all_gather x1, waiting for transfers between devices, body(): shard_piece = lax.all_gather(grad_pre, 'feat', axis=0, tiled=True)  26.3 us
    gather x1, local copies, waits for them, and re-layouts, body(): own = jnp.take(feature_rows, target_ids[0], axis=1)  13.8 us
    unnamed x22, local copies, waits for them, and re-layouts  11.6 us
    dot_general x4, matrix products, contract_first(): lax.dot_general(left, right, (((0,), (1,)), ((), ())), preferred_element_...  10.2 us
  transfers between devices with their start and end apart: 4, of which 4 were waited for; matrix products, arithmetic and copies ran while one was open for 4% of the time, Pallas kernels for 0%

commit v1 on v0

--- a/solution.py
+++ b/solution.py
@@ -49,7 +49,25 @@
     grad_hidden = jnp.dot(cotangent, w_head, preferred_element_type=jnp.float32)
     sigma = jax.nn.sigmoid(preact)
     grad_pre = (grad_hidden * sigma * (1.0 + preact * (1.0 - sigma))).astype(jnp.bfloat16)
-    shard_piece = lax.all_gather(grad_pre, "feat", axis=0, tiled=True)
+    length, index, span = (lax.axis_size("feat"), lax.axis_index("feat"), grad_pre.shape[0])
+    ahead = [(i, (i + 1) % length) for i in range(length)]
+    backward = [(i, (i - 1) % length) for i in range(length)]
+    shard_piece = jnp.zeros(
+        (*grad_pre.shape[:0], length * span, *grad_pre.shape[0 + 1 :]), grad_pre.dtype
+    )
+    shard_piece = lax.dynamic_update_slice_in_dim(shard_piece, grad_pre, index * span, axis=0)
+    from_left = from_right = grad_pre
+    middle = length // 2
+    for step in range(1, middle + 1):
+        from_left = lax.ppermute(from_left, "feat", ahead)
+        shard_piece = lax.dynamic_update_slice_in_dim(
+            shard_piece, from_left, (index - step) % length * span, axis=0
+        )
+        if step < length - middle:
+            from_right = lax.ppermute(from_right, "feat", backward)
+            shard_piece = lax.dynamic_update_slice_in_dim(
+                shard_piece, from_right, (index + step) % length * span, axis=0
+            )
     agg_part = aggregate
     own_part = own
     neigh_local = contract_first(shard_piece, agg_part)

time: 309 us -> 289 us (0.935)
  waiting for transfers between devices: 240 us -> 210 us
  starting transfers between devices: 0.16 us -> 8.11 us
  local copies, waits for them, and re-layouts: 30 us -> 35.9 us
  matrix products: 21 us -> 16.7 us
    all_gather x1 -> x0, waiting for transfers between devices: 26.3 us -> none  [body(): shard_piece = lax.all_gather(grad_pre, 'feat', axis=0, tiled=True)]
    psum x1, waiting for transfers between devices: 125 us -> 99.9 us  [body(): grad_head = lax.psum(head_local, ('feat', 'node'))]
    ppermute x0 -> x7, waiting for transfers between devices: none -> 20.9 us  [the longest x4 20.9 us: body(): from_left = lax.ppermute(from_left, 'feat', ahead)]
    ppermute x0 -> x7, starting transfers between devices: none -> 7.99 us  [the longest x3 7.98 us: body(): from_right = lax.ppermute(from_right, 'feat', backward)]
    dynamic_update_slice x0 -> x7, local copies, waits for them, and re-layouts: none -> 3.96 us  [the longest x4 1.99 us: body(): lax.dynamic_update_slice_in_dim(shard_piece, from_left, (index - step) %...]
    dot_general x4, matrix products: 10.2 us -> 6.99 us  [contract_first(): lax.dot_general(left, right, (((0,), (1,)), ((), ())), preferred_element_...]
    unnamed x22 -> x26, local copies, waits for them, and re-layouts: 11.6 us -> 13.4 us
  transfers between devices with their start and end apart: 4 -> 10, of which waited for: 4 -> 7; matrix products, arithmetic and copies ran while one was open for 4% -> 4% of each run, Pallas kernels for 0% -> 0%
where the time goes in v1:
time: 289 us; the launch traced here: 288 us
  waiting for transfers between devices  210 us (73%)
  local copies, waits for them, and re-layouts  35.9 us (12%)
  matrix products  16.7 us (6%)
  between operations  14 us (5%)
  starting transfers between devices  8.11 us (3%)
  other arithmetic  3.59 us (1%)
    psum x1, waiting for transfers between devices, body(): grad_head = lax.psum(head_local, ('feat', 'node'))  99.9 us
    reduce_scatter x1, waiting for transfers between devices, body(): lax.psum_scatter(contract_first(agg_part, w_neigh) + contract_first(own_p...  54.1 us
    psum x1, waiting for transfers between devices, body(): grad_neigh, grad_self = lax.psum((neigh_local, self_local), 'node')  34.9 us
    ppermute x4, waiting for transfers between devices, body(): from_left = lax.ppermute(from_left, 'feat', ahead)  20.9 us
    gather x1, local copies, waits for them, and re-layouts, body(): own = jnp.take(feature_rows, target_ids[0], axis=1)  13.8 us
    unnamed x26, local copies, waits for them, and re-layouts  13.4 us
    ppermute x3, starting transfers between devices, body(): from_right = lax.ppermute(from_right, 'feat', backward)  7.98 us
    dot_general x4, matrix products, contract_first(): lax.dot_general(left, right, (((0,), (1,)), ((), ())), preferred_element_...  6.99 us
  transfers between devices with their start and end apart: 10, of which 7 were waited for; matrix products, arithmetic and copies ran while one was open for 4% of the time, Pallas kernels for 0%

profile of v1, /device:TPU:0, one launch (start us, length us, event | category | flops | bytes accessed | tf_op | source)
XLA Modules:
  0.0 288.0 jit_solution(17288149852076742208)
XLA Ops:
  7.2 0.0 reduce-scatter.2.cloned.1.call-start
  7.2 0.7 compare_and_fusion.1
  8.0 0.8 copy.23
  8.7 0.7 bitcast_convert_fusion
  9.4 0.1 copy.22
  9.5 0.7 compare_select_fusion
  10.2 0.7 compare_and_fusion
  10.9 0.7 fusion.33
  11.7 0.1 reshape_squeeze.10
  11.8 4.9 %copy.26 = bf16[1,64,16384]{1,2,0:T(8,128)(2,1)} copy(bf16[1,64,16384]{2,1,0:T(8,128)(2,1)} %param.9) | data formatting | bytes 4194304 | tf_op args[0]
  16.7 0.6 copy.30
  17.3 1.4 copy.24
  18.7 3.1 %gather_fusion = bf16[256,64,128]{2,1,0:T(8,128)(2,1)} fusion(bf16[64,128,128]{2,0,1:T(8,128)(2,1)S(1)} %copy.24, s32[1024]{0:T(1024)S(1)} %pad_clamp_fusion), kind=kCustom, calls=%fused_computation | custom fusion | bytes 8389632 | tf_op jit(solution)/shard_map/jit(_take)/gather | solution.py:12
  21.8 13.8 %gather_fusion.1 = bf16[4096,64]{1,0:T(8,128)(2,1)S(1)} fusion(bf16[64,16384]{0,1:T(8,128)(2,1)} %bitcast.59, s32[4096]{0:T(1024)S(1)} %broadcast_clamp_fusion), kind=kCustom, calls=%fused_computation.1 | custom fusion | bytes 1064960 | tf_op jit(solution)/shard_map/jit(_take)/gather | solution.py:33
  35.6 1.5 fusion.29
  37.0 0.7 copy-done.2
  37.7 5.6 %fusion.19 = bf16[32,8,8,128]{3,2,1,0:T(8,128)(2,1)S(1)} fusion(bf16[1,32,8,128,128]{4,3,2,1,0:T(8,128)(2,1)} %param.13, bf16[64,32,8,128]{3,0,2,1:T(8,128)(2,1)S(1)} %bitcast.62, pred[32,8]{1,0:T(8,128)(4,1)S(1)} %copy.22, bf16[32,8]{1,0:T(8,128)(2,1)S(1)} %fusion.33, f32[32]{0:T(128)S(1)} %bitcast_convert_fusion), kind=kOutput, calls=%fused_computation.19 | convolution fusion | flops 541589504 | bytes 13108096 | tf_op jit(solution)/shard_map/tkrs,ftks->ftr/dot_general | solution.py:15
  43.4 0.8 copy-done.3
  44.2 2.7 convolution_add_fusion
  46.9 0.0 reduce-scatter.2.cloned.1.call-update
  46.9 0.0 all-reduce.4.cloned.1.call-start
  46.9 54.1 %reduce-scatter.2.cloned.1.call-done = f32[512,256]{1,0:T(8,128)} async-done(((f32[4096,256]{1,0:T(8,128)}), f32[512,256]{1,0:T(8,128)}) %reduce-scatter.2.cloned.1.call-update) | async-done | bytes 524304 | tf_op jit(solution)/shard_map/reduce_scatter | solution.py:36
  101.0 0.1 broadcast_in_dim.34
  101.2 0.9 copy-done.7
  102.1 1.0 constant_dynamic-update-slice_fusion.7
  103.1 2.6 collective-permute-start.1
  105.7 6.4 %collective-permute-done = bf16[512,256]{1,0:T(8,128)(2,1)} collective-permute-done((bf16[512,256]{1,0:T(8,128)(2,1)}, bf16[512,256]{1,0:T(8,128)(2,1)}, u32[]{:S(2)}, u32[]{:S(2)}) %collective-permute-start) | collective-permute-done | bytes 262176 | tf_op jit(solution)/shard_map/ppermute | solution.py:62
  112.1 2.6 collective-permute-start.3
  114.7 2.1 convolution_bitcast_fusion
  116.8 0.0 all-reduce.4.cloned.1.call-update
  116.8 0.0 all-reduce.6.cloned.1.call-start
  116.9 4.8 %collective-permute-done.2 = bf16[512,256]{1,0:T(8,128)(2,1)} collective-permute-done((bf16[512,256]{1,0:T(8,128)(2,1)}, bf16[512,256]{1,0:T(8,128)(2,1)}, u32[]{:S(2)}, u32[]{:S(2)}) %collective-permute-start.2) | collective-permute-done | bytes 262176 | tf_op jit(solution)/shard_map/ppermute | solution.py:62
  121.7 1.0 constant_dynamic-update-slice_fusion.6
  122.7 1.0 constant_dynamic-update-slice_fusion.5
  123.7 2.7 collective-permute-start.5
  126.3 1.0 constant_dynamic-update-slice_fusion.4
  127.3 4.0 %collective-permute-done.4 = bf16[512,256]{1,0:T(8,128)(2,1)S(1)} collective-permute-done((bf16[512,256]{1,0:T(8,128)(2,1)}, bf16[512,256]{1,0:T(8,128)(2,1)S(1)}, u32[]{:S(2)}, u32[]{:S(2)}) %collective-permute-start.4) | collective-permute-done | bytes 262176 | tf_op jit(solution)/shard_map/ppermute | solution.py:62
  131.3 1.0 constant_dynamic-update-slice_fusion.3
  132.3 5.7 %collective-permute-done.6 = bf16[512,256]{1,0:T(8,128)(2,1)S(1)} collective-permute-done((bf16[512,256]{1,0:T(8,128)(2,1)S(1)}, bf16[512,256]{1,0:T(8,128)(2,1)S(1)}, u32[]{:S(2)}, u32[]{:S(2)}) %collective-permute-start.6) | collective-permute-done | bytes 262176 | tf_op jit(solution)/shard_map/ppermute | solution.py:62
  138.1 1.7 fusion.30
  139.8 1.1 fusion.24
  140.9 0.0 all-reduce.6.cloned.1.call-update
  141.0 1.0 fusion.14
  142.0 99.9 %all-reduce.4.cloned.1.call-done = f32[256,256]{0,1:T(8,128)} async-done(((f32[256,256]{0,1:T(8,128)}), f32[256,256]{0,1:T(8,128)}) %all-reduce.4.cloned.1.call-update) | async-done | bytes 262160 | tf_op jit(solution)/shard_map/psum | solution.py:48
  241.9 1.8 copy.27
  243.7 34.9 %all-reduce.6.cloned.1.call-done = (f32[256,64]{0,1:T(8,128)}, f32[256,64]{0,1:T(8,128)}) async-done(((f32[256,64]{0,1:T(8,128)}, f32[256,64]{0,1:T(8,128)}), (f32[256,64]{0,1:T(8,128)}, f32[256,64]{0,1:T(8,128)})) %all-reduce.6.cloned.1.call-update) | async-done | bytes 131088 | tf_op jit(solution)/shard_map/psum | solution.py:75
  278.6 1.5 copy.50
  280.0 1.5 copy.51
  (30 shorter events, 0.1 us)
Async XLA Ops:
  7.2 94.0 %copy-start = (bf16[1,512,256]{2,1,0:T(8,128)(2,1)S(1)}, bf16[1,512,256]{2,1,0:T(8,128)(2,1)}, u32[]{:S(2)}) copy-start(bf16[1,512,256]{2,1,0:T(8,128)(2,1)} %param.17) | copy-start | bytes 786436
  7.2 93.9 %reduce-scatter.2.cloned.1.call-start = ((), (), s32[]{:S(2)}) async-start(), calls=%async_computation.1 | async-start | bytes 4718592 | tf_op jit(solution)/shard_map/reduce_scatter | solution.py:36
  11.8 5.0 %copy-start.1 = (bf16[1,64,16384]{2,1,0:T(8,128)(2,1)S(1)}, bf16[1,64,16384]{2,1,0:T(8,128)(2,1)}, u32[]{:S(2)}) copy-start(bf16[1,64,16384]{2,1,0:T(8,128)(2,1)} %param.9) | copy-start | bytes 6291460
  21.8 13.8 %copy-start.5 = (bf16[256,64]{0,1:T(8,128)(2,1)S(1)}, bf16[256,64]{0,1:T(8,128)(2,1)}, u32[]{:S(2)}) copy-start(bf16[256,64]{0,1:T(8,128)(2,1)} %param.15) | copy-start | bytes 98308
  35.5 2.2 copy-start.2
  37.7 6.4 %copy-start.6 = (bf16[256,64]{0,1:T(8,128)(2,1)S(1)}, bf16[256,64]{0,1:T(8,128)(2,1)}, u32[]{:S(2)}) copy-start(bf16[256,64]{0,1:T(8,128)(2,1)} %param.14) | copy-start | bytes 98308
  43.4 0.8 copy-start.3
  46.9 54.3 %copy-start.9 = (bf16[256,256]{1,0:T(8,128)(2,1)S(1)}, bf16[256,256]{1,0:T(8,128)(2,1)}, u32[]{:S(2)}) copy-start(bf16[256,256]{1,0:T(8,128)(2,1)} %param.16) | copy-start | bytes 393220
  46.9 195.0 %all-reduce.4.cloned.1.call-start = ((), (), s32[]{:S(2)}) async-start(), calls=%async_computation.2 | async-start | bytes 524288 | tf_op jit(solution)/shard_map/psum | solution.py:48
  101.0 1.0 copy-start.7
  103.1 9.0 %collective-permute-start = (bf16[512,256]{1,0:T(8,128)(2,1)}, bf16[512,256]{1,0:T(8,128)(2,1)}, u32[]{:S(2)}, u32[]{:S(2)}) collective-permute-start(bf16[512,256]{1,0:T(8,128)(2,1)} %get-tuple-element.19), channel_id=1, source_target_pairs={{0,4},{4,8},{8,12},{12,16},{16,20},{20,24},{24,28},{28,0},{1,5},{5... | collective-permute-start | bytes 786440 | tf_op jit(solution)/shard_map/ppermute | solution.py:62
  103.1 9.0 %collective-permute-start.1 = (bf16[512,256]{1,0:T(8,128)(2,1)}, bf16[512,256]{1,0:T(8,128)(2,1)}, u32[]{:S(2)}, u32[]{:S(2)}) collective-permute-start(bf16[512,256]{1,0:T(8,128)(2,1)} %get-tuple-element.19), channel_id=1, source_target_pairs={{0,28},{4,0},{8,4},{12,8},{16,12},{20,16},{24,20},{28,24},{1,29},{... | collective-permute-start | bytes 786440 | tf_op jit(solution)/shard_map/ppermute | solution.py:67
  112.1 9.6 %collective-permute-start.2 = (bf16[512,256]{1,0:T(8,128)(2,1)}, bf16[512,256]{1,0:T(8,128)(2,1)}, u32[]{:S(2)}, u32[]{:S(2)}) collective-permute-start(bf16[512,256]{1,0:T(8,128)(2,1)} %collective-permute-done), channel_id=1, source_target_pairs={{0,4},{4,8},{8,12},{12,16},{16,20},{20,24},{24,28},{28,0},{1,5},{5... | collective-permute-start | bytes 786440 | tf_op jit(solution)/shard_map/ppermute | solution.py:62
  112.1 11.6 %collective-permute-start.3 = (bf16[512,256]{1,0:T(8,128)(2,1)}, bf16[512,256]{1,0:T(8,128)(2,1)}, u32[]{:S(2)}, u32[]{:S(2)}) collective-permute-start(bf16[512,256]{1,0:T(8,128)(2,1)} %collective-permute-done.1), channel_id=1, source_target_pairs={{0,28},{4,0},{8,4},{12,8},{16,12},{20,16},{24,20},{28,24},{1,29},{... | collective-permute-start | bytes 786440 | tf_op jit(solution)/shard_map/ppermute | solution.py:67
  116.8 161.7 %all-reduce.6.cloned.1.call-start = ((), (), s32[]{:S(2)}) async-start(), calls=%async_computation.3 | async-start | bytes 262144 | tf_op jit(solution)/shard_map/psum | solution.py:75
  121.7 9.6 %collective-permute-start.4 = (bf16[512,256]{1,0:T(8,128)(2,1)}, bf16[512,256]{1,0:T(8,128)(2,1)S(1)}, u32[]{:S(2)}, u32[]{:S(2)}) collective-permute-start(bf16[512,256]{1,0:T(8,128)(2,1)} %collective-permute-done.2), channel_id=1, source_target_pairs={{0,4},{4,8},{8,12},{12,16},{16,20},{20,24},{24,28},{28,0},{1,5},{5... | collective-permute-start | bytes 786440 | tf_op jit(solution)/shard_map/ppermute | solution.py:62
  123.7 8.6 %collective-permute-start.5 = (bf16[512,256]{1,0:T(8,128)(2,1)}, bf16[512,256]{1,0:T(8,128)(2,1)S(1)}, u32[]{:S(2)}, u32[]{:S(2)}) collective-permute-start(bf16[512,256]{1,0:T(8,128)(2,1)} %collective-permute-done.3), channel_id=1, source_target_pairs={{0,28},{4,0},{8,4},{12,8},{16,12},{20,16},{24,20},{28,24},{1,29},{... | collective-permute-start | bytes 786440 | tf_op jit(solution)/shard_map/ppermute | solution.py:67
  131.3 6.8 %collective-permute-start.6 = (bf16[512,256]{1,0:T(8,128)(2,1)S(1)}, bf16[512,256]{1,0:T(8,128)(2,1)S(1)}, u32[]{:S(2)}, u32[]{:S(2)}) collective-permute-start(bf16[512,256]{1,0:T(8,128)(2,1)S(1)} %collective-permute-done.4), channel_id=1, source_target_pairs={{0,4},{4,8},{8,12},{12,16},{16,20},{20,24},{24,28},{28,0},{1,5},{5... | collective-permute-start | bytes 786440 | tf_op jit(solution)/shard_map/ppermute | solution.py:62
  138.1 1.7 copy-start.4
  139.8 1.1 copy-start.8
Sparse Core Ops, SparseCore 0:
  47.0 53.9 reduce-scatter.1
  117.0 124.8 all-reduce.3
  245.0 33.5 all-reduce.5
